TPU v7x, 32 devices: a whole 2x2x4 slice. The times are simulated.
32 devices in a mesh: dp: 4 (over y, x), expert: 8 (over z, core).
Axes of the slice: x: 2, y: 2, z: 4, core: 2. Of those that a mesh axis runs over, the one named last changes fastest.
Arguments:
- grad_out: bfloat16 [4096, 5120], P(('dp', 'expert')), may hold values from -6 to 6
- expert_ids: int32 [4096, 1], P(('dp', 'expert')), may hold values from 0 to 7; in each aligned block of 128 rows (0 to 127, 128 to 255, ...) at most 20 rows name the same one
- gate_weights: bfloat16 [4096], P(('dp', 'expert')), may hold values from 0.099609375 to 1
- saved_hidden: bfloat16 [8, 640, 8192], P('expert', None, 'dp'), may hold values from -0.06591797 to 0.06591797
- down_weight: bfloat16 [8, 8192, 5120], P('expert', 'dp'), may hold values from -0.0625 to 0.0625
Outputs:
- grad_hidden: bfloat16 [8, 640, 8192], P('expert', None, 'dp')
- grad_gate: float32 [4096], P(('dp', 'expert'))
Inputs may be any that keep to these rules, and one draw needn't show every extreme that they name: `expert_ids`: within the 128 tokens of one device no expert is named more than 20 times, and in every draw some expert is named exactly 20 times by some device's tokens.
All inputs are finite; a program needn't handle non-finite values.
Results may differ from a plain program's by a relative error of at most 0.001.
Values may be sent and summed in bfloat16 or wider, within the bound.
A program may use at most 192 MiB of HBM per device.

v0:
```python
import jax
import jax.numpy as jnp
from jax import lax
from jax.sharding import PartitionSpec as P


def shards(grad_out, expert_ids, gate_weights, saved_hidden, down_weight):
    experts_here = lax.axis_size("expert")
    width = grad_out.shape[1]
    tok_rows = grad_out.shape[0]
    most = tok_rows * 5 // (4 * experts_here)
    chosen = expert_ids[:, 0]
    onehot = (chosen[:, None] == jnp.arange(experts_here, dtype=jnp.int32)[None, :]).astype(
        jnp.int32
    )
    earlier = jnp.cumsum(onehot, axis=0) - onehot
    slot = jnp.sum(earlier * onehot, axis=1)
    target = chosen * most + slot
    placing = jnp.arange(experts_here * most, dtype=jnp.int32)[:, None] == target[None, :]
    placing_bf = placing.astype(jnp.bfloat16)
    send_rows = jnp.dot(placing_bf, grad_out, preferred_element_type=jnp.float32).astype(
        jnp.bfloat16
    )
    send_rows = send_rows.reshape(experts_here, most, width)
    send_gates = jnp.dot(placing_bf, gate_weights[:, None], preferred_element_type=jnp.float32)
    send_gates = send_gates.astype(jnp.bfloat16).reshape(experts_here, most)
    landed_rows, landed_gates = (
        lax.all_to_all(send_rows, "expert", split_axis=0, concat_axis=0, tiled=True),
        lax.all_to_all(send_gates, "expert", split_axis=0, concat_axis=0, tiled=True),
    )
    arrived, arrived_gates = (
        lax.all_gather(landed_rows[None], "dp", axis=0, tiled=True),
        lax.all_gather(landed_gates[None], "dp", axis=0, tiled=True),
    )
    flat_rows = arrived.reshape(-1, width)
    flat_gates = arrived_gates.reshape(-1).astype(jnp.float32)
    back = lax.dot_general(
        flat_rows, down_weight[0], (((1,), (1,)), ((), ())), preferred_element_type=jnp.float32
    )
    grad_hidden = (flat_gates[:, None] * back).astype(jnp.bfloat16)[None]
    partial_gate = jnp.sum(saved_hidden[0].astype(jnp.float32) * back, axis=1)
    share_len = experts_here * most
    total_gate = lax.psum(partial_gate, "dp")
    own_gate = lax.dynamic_slice_in_dim(total_gate, lax.axis_index("dp") * share_len, share_len, 0)
    returned = lax.all_to_all(
        own_gate.reshape(experts_here, most), "expert", split_axis=0, concat_axis=0, tiled=True
    )
    grad_gate = jnp.sum(placing.astype(jnp.float32) * returned.reshape(-1)[:, None], axis=0)
    return (grad_hidden, grad_gate)


def solution(mesh):
    in_specs = (
        P(("dp", "expert"), None),
        P(("dp", "expert"), None),
        P(("dp", "expert")),
        P("expert", None, "dp"),
        P("expert", "dp", None),
    )
    out_specs = (P("expert", None, "dp"), P(("dp", "expert")))
    return jax.shard_map(shards, mesh=mesh, in_specs=in_specs, out_specs=out_specs, check_vma=False)
```

profile of v0, /device:TPU:0, one launch (start us, length us, event | category | flops | bytes accessed | tf_op | source)
XLA Modules:
  0.0 206.5 jit_solution(11658039345238599644)
XLA Ops:
  7.2 0.0 copy-start
  7.2 0.0 all-gather.4.cloned.1.call-start
  7.2 0.8 fusion.5
  8.1 0.2 reduce_window_sum.11
  8.2 0.8 select_reduce_fusion.1
  9.1 0.7 multiply_add_fusion
  9.7 0.0 copy-done
  9.7 1.7 convolution_convert_fusion
  11.5 1.6 reshape.44
  13.1 0.0 copy-start.1
  13.1 52.4 %all_to_all.24 = bf16[8,20,5120]{2,1,0:T(8,128)(2,1)S(1)} all-to-all(bf16[8,20,5120]{2,1,0:T(8,128)(2,1)S(1)} %reshape.44), channel_id=1, replica_groups=mesh['dp'=4,'expert'=8] {'expert'}, dimensions={0} | all-to-all | bytes 3276800 | tf_op jit(solution)/shard_map/all_to_all | solution.py:28
  65.5 2.1 copy.16
  67.5 0.0 all-gather.4.cloned.1.call-update
  67.6 0.0 copy-done.1
  67.6 0.1 fusion.4
  67.7 0.7 all_to_all.20
  68.4 3.3 %all-to-all-start = ((bf16[8,1,20]{2,1,0:T(2,128)(2,1)}), bf16[8,1,20]{2,1,0:T(2,128)(2,1)S(1)}, u32[]{:S(2)}, u32[]{:S(2)}) async-start(bf16[8,1,20]{2,1,0:T(2,128)(2,1)} %all_to_all.20), calls=%async_computation | async-start | bytes 8192 | tf_op jit(solution)/shard_map/all_to_all | solution.py:29
  71.8 5.5 %all-to-all-done = bf16[8,1,20]{2,1,0:T(2,128)(2,1)S(1)} async-done(((bf16[8,1,20]{2,1,0:T(2,128)(2,1)}), bf16[8,1,20]{2,1,0:T(2,128)(2,1)S(1)}, u32[]{:S(2)}, u32[]{:S(2)}) %all-to-all-start) | async-done | bytes 352 | tf_op jit(solution)/shard_map/all_to_all | solution.py:29
  77.3 8.1 %all-gather = bf16[32,1,20]{2,0,1:T(8,128)(2,1)S(1)} all-gather(bf16[8,1,20]{2,0,1:T(8,128)(2,1)S(1)} %copy.15), channel_id=2, replica_groups=mesh['dp'=4,'expert'=8] {'dp'}, dimensions={0}, use_global_device_ids=true | all-gather | bytes 1600 | tf_op jit(solution)/shard_map/all_gather | solution.py:33
  85.3 0.1 reshape.46
  85.4 53.6 %all-gather.4.cloned.1.call-done = bf16[32,20,5120]{2,0,1:T(8,128)(2,1)} async-done(((bf16[8,20,5120]{2,0,1:T(8,128)(2,1)}), bf16[32,20,5120]{2,0,1:T(8,128)(2,1)}) %all-gather.4.cloned.1.call-update) | async-done | bytes 6553616 | tf_op jit(solution)/shard_map/all_gather | solution.py:32
  139.0 9.6 %copy.17 = bf16[32,20,5120]{2,1,0:T(8,128)(2,1)} copy(bf16[32,20,5120]{2,0,1:T(8,128)(2,1)} %all-gather.4.cloned.1.call-done) | data formatting | bytes 13107200 | tf_op jit(solution)/shard_map/all_gather | solution.py:32
  148.6 8.7 %reshape.45 = bf16[640,5120]{1,0:T(8,128)(2,1)} reshape(bf16[32,20,5120]{2,1,0:T(8,128)(2,1)} %copy.17) | data formatting | bytes 13107200 | tf_op jit(solution)/shard_map/reshape | solution.py:35
  157.3 21.4 %fusion.2 = (f32[640]{0:T(1024)S(1)}, bf16[1,640,2048]{2,1,0:T(8,128)(2,1)}) fusion(bf16[1,640,2048]{2,1,0:T(8,128)(2,1)} %param.8, f32[640]{0:T(1024)S(1)} %reshape.46, bf16[640,5120]{1,0:T(8,128)(2,1)} %reshape.45, bf16[1,2048,5120]{2,1,0:T(8,128)(2,1)} %param.9), kind=kOutput, calls=%fused_computation.4 | convolution fusion | flops 13428325376 | bytes 32773120 | tf_op jit(solution)/shard_map/dot_general | solution.py:37
  178.7 8.9 %psum.7 = f32[640]{0:T(1024)S(1)} all-reduce(f32[640]{0:T(1024)S(1)} %get-tuple-element.2), channel_id=1, replica_groups=mesh['dp'=4,'expert'=8] {'dp'}, use_global_device_ids=true, to_apply=%region_3.4 | all-reduce | flops 640 | bytes 5120 | tf_op jit(solution)/shard_map/psum | solution.py:43
  187.6 0.1 dynamic_slice.3
  187.7 0.1 all_to_all.18
  187.8 9.9 %all_to_all.25 = f32[8,1,20]{2,1,0:T(1,128)S(1)} all-to-all(f32[8,1,20]{2,1,0:T(1,128)S(1)} %all_to_all.18), channel_id=1, replica_groups=mesh['dp'=4,'expert'=8] {'expert'}, dimensions={0} | all-to-all | bytes 1280 | tf_op jit(solution)/shard_map/all_to_all | solution.py:45
  197.7 0.5 broadcast.17
  198.2 0.7 reduce.3
  198.9 0.1 mul.44
  199.0 0.6 select_reduce_fusion
  (2 shorter events, 0.0 us)
Async XLA Ops:
  7.2 2.6 %copy-start = (bf16[128,5120]{1,0:T(8,128)(2,1)S(1)}, bf16[128,5120]{1,0:T(8,128)(2,1)}, u32[]{:S(2)}) copy-start(bf16[128,5120]{1,0:T(8,128)(2,1)} %param.5) | copy-start | bytes 3932164
  7.2 131.8 %all-gather.4.cloned.1.call-start = ((), (), s32[]{:S(2)}) async-start(), calls=%async_computation.3 | async-start | bytes 8192000 | tf_op jit(solution)/shard_map/all_gather | solution.py:32
  13.1 54.5 %copy-start.1 = (bf16[128]{0:T(256)(128)(2,1)S(1)}, bf16[128]{0:T(256)(128)(2,1)}, u32[]{:S(2)}) copy-start(bf16[128]{0:T(256)(128)(2,1)} %param.7) | copy-start | bytes 772
  68.4 8.8 %all-to-all-start = ((bf16[8,1,20]{2,1,0:T(2,128)(2,1)}), bf16[8,1,20]{2,1,0:T(2,128)(2,1)S(1)}, u32[]{:S(2)}, u32[]{:S(2)}) async-start(bf16[8,1,20]{2,1,0:T(2,128)(2,1)} %all_to_all.20), calls=%async_computation | async-start | bytes 8192 | tf_op jit(solution)/shard_map/all_to_all | solution.py:29
Sparse Core Ops, SparseCore 0:
  67.7 71.2 all-gather.3
where the time goes:
time: 207 us; the launch traced here: 206 us
  blocking collectives  79.3 us (38%)
  waiting for transfers between devices  59.1 us (29%)
  local copies, waits for them, and re-layouts  23.5 us (11%)
  matrix products  23.3 us (11%)
  between operations  14.1 us (7%)
  other arithmetic  3.78 us (2%)
  starting transfers between devices  3.37 us (2%)
    all_gather x1, waiting for transfers between devices, shards(): lax.all_gather(landed_rows[None], 'dp', axis=0, tiled=True)  53.6 us
    all_to_all x1, blocking collectives, shards(): lax.all_to_all(send_rows, 'expert', split_axis=0, concat_axis=0, tiled=True)  52.4 us
    dot_general x1, matrix products, shards(): lax.dot_general(flat_rows, down_weight[0], (((1,), (1,)), ((), ())), pref...  21.4 us
    all_to_all x1, blocking collectives, shards(): lax.all_to_all(own_gate.reshape(experts_here, most), 'expert', split_axis...  9.94 us
    all_gather x1, local copies, waits for them, and re-layouts, shards(): lax.all_gather(landed_rows[None], 'dp', axis=0, tiled=True)  9.63 us
    psum x1, blocking collectives, shards(): total_gate = lax.psum(partial_gate, 'dp')  8.92 us
    reshape x1, local copies, waits for them, and re-layouts, shards(): flat_rows = arrived.reshape(-1, width)  8.66 us
    all_gather x1, blocking collectives, shards(): lax.all_gather(landed_gates[None], 'dp', axis=0, tiled=True)  8.08 us
  transfers between devices with their start and end apart: 2, of which 2 were waited for; matrix products, arithmetic and copies ran while one was open for 0% of the time, Pallas kernels for 0%

commit v1 on v0

v1 whole, which is shorter than its diff:
```python
import functools
import math

import jax
import jax.numpy as jnp
from jax import lax
from jax.experimental import pallas as pl
from jax.experimental.pallas import tpu as pltpu
from jax.sharding import PartitionSpec as P

MESH = pl.DeviceIdType.MESH
F32 = jnp.float32
BF16 = jnp.bfloat16
LANES = 128
NT = (((1,), (1,)), ((), ()))


def flip(index, mask):
    out, bit = index, 1
    while bit <= mask:
        if mask & bit:
            out = out + bit * (1 - 2 * ((index // bit) % 2))
        bit *= 2
    return out


def kernel(
    dps, exps, most, parts,
    grad_hbm, ids_ref, gate_ref, hid_hbm, w_hbm,
    out_hbm, gg_ref,
    tokens, w, hid, ostage, send, raw, gsend, gts, x, gacc, psend_buf, precv_buf, total, ret,
    load_sem, out_sem, zs, zr, gzs, gzr, ps, pr, gps, gpr, rs, rr, ts, tr,
):
    d = lax.axis_index("dp")
    e = lax.axis_index("expert")
    toks = grad_hbm.shape[0]
    width = grad_hbm.shape[1]
    cols = width // parts
    block = parts * most
    rows = exps * most
    units = w.shape[0]

    loads = [
        pltpu.make_async_copy(
            grad_hbm.at[:, pl.ds(q * cols, cols)],
            tokens.at[pl.ds(q * toks, toks), :],
            load_sem.at[q],
        )
        for q in range(parts)
    ]
    loads.append(pltpu.make_async_copy(w_hbm, w, load_sem.at[parts]))
    loads.append(pltpu.make_async_copy(hid_hbm, hid, load_sem.at[parts + 1]))
    for copy in loads:
        copy.start()

    barrier = pltpu.get_barrier_semaphore()
    for k in range(1, exps):
        pl.semaphore_signal(barrier, inc=1, device_id=(d, flip(e, k)), device_id_type=MESH)
    for k in range(1, dps):
        pl.semaphore_signal(barrier, inc=1, device_id=(flip(d, k), e), device_id_type=MESH)

    ids = ids_ref[...]
    onehot = (lax.broadcasted_iota(jnp.int32, (exps, toks), 0) == ids).astype(F32)
    before = (
        lax.broadcasted_iota(jnp.int32, (toks, toks), 0)
        < lax.broadcasted_iota(jnp.int32, (toks, toks), 1)
    )
    earlier = jnp.dot(
        onehot.astype(BF16), before.astype(F32).astype(BF16), preferred_element_type=F32
    )
    slot = jnp.sum(earlier * onehot, axis=0, keepdims=True).astype(jnp.int32)
    target = ids * most + slot

    r4 = lax.broadcasted_iota(jnp.int32, (block, parts * toks), 0)
    c4 = lax.broadcasted_iota(jnp.int32, (block, parts * toks), 1)
    same_part = (r4 // most) == (c4 // toks)
    r_slot = r4 % most
    target4 = jnp.concatenate([target] * parts, axis=1)
    lane_slot = lax.broadcasted_iota(jnp.int32, (LANES, toks), 0)
    gate_rows = jnp.broadcast_to(gate_ref[...].astype(F32), (16, toks)).astype(BF16)

    def block_for(dest):
        place = jnp.where(same_part & (r_slot + dest * most == target4), 1.0, 0.0).astype(BF16)
        return jnp.dot(place, tokens[...], preferred_element_type=F32).astype(BF16)

    def gates_for(dest):
        hit = (lane_slot < most) & (lane_slot + dest * most == target)
        place = jnp.where(hit, 1.0, 0.0).astype(BF16)
        return lax.dot_general(gate_rows, place, NT, preferred_element_type=F32).astype(BF16)

    def z_copy(k):
        dest = flip(e, k)
        return pltpu.make_async_remote_copy(
            src_ref=send.at[k], dst_ref=raw.at[d, e], send_sem=zs.at[k], recv_sem=zr.at[e],
            device_id=(d, dest), device_id_type=MESH,
        )

    def z_gate(k):
        dest = flip(e, k)
        return pltpu.make_async_remote_copy(
            src_ref=gsend.at[k], dst_ref=gts.at[d, e], send_sem=gzs.at[k], recv_sem=gzr.at[e],
            device_id=(d, dest), device_id_type=MESH,
        )

    def plane_copy(of, via, k, j):
        s = flip(e, k)
        src = flip(d, of)
        return pltpu.make_async_remote_copy(
            src_ref=raw.at[src, s], dst_ref=raw.at[src, s], send_sem=ps.at[j, k],
            recv_sem=pr.at[src, s], device_id=(flip(d, via), e), device_id_type=MESH,
        )

    def z_wait(k):
        s = flip(e, k)
        pltpu.make_async_remote_copy(
            src_ref=send.at[k], dst_ref=raw.at[d, s], send_sem=zs.at[k], recv_sem=zr.at[s],
            device_id=(d, s), device_id_type=MESH,
        ).wait_recv()

    def gate_wait(k):
        s = flip(e, k)
        pltpu.make_async_remote_copy(
            src_ref=gsend.at[k], dst_ref=gts.at[d, s], send_sem=gzs.at[k], recv_sem=gzr.at[s],
            device_id=(d, s), device_id_type=MESH,
        ).wait_recv()

    def plane_gate(k):
        return pltpu.make_async_remote_copy(
            src_ref=gts.at[d], dst_ref=gts.at[d], send_sem=gps.at[k], recv_sem=gpr.at[d],
            device_id=(flip(d, k), e), device_id_type=MESH,
        )

    def plane_gate_wait(k):
        src = flip(d, k)
        pltpu.make_async_remote_copy(
            src_ref=gts.at[d], dst_ref=gts.at[src], send_sem=gps.at[k], recv_sem=gpr.at[src],
            device_id=(src, e), device_id_type=MESH,
        ).wait_recv()

    def sum_copy(k):
        return pltpu.make_async_remote_copy(
            src_ref=psend_buf.at[k], dst_ref=precv_buf.at[k], send_sem=rs.at[k],
            recv_sem=rr.at[k], device_id=(flip(d, k), e), device_id_type=MESH,
        )

    def back_copy(k):
        return pltpu.make_async_remote_copy(
            src_ref=total, dst_ref=ret.at[k], send_sem=ts.at[k], recv_sem=tr.at[k],
            device_id=(d, flip(e, k)), device_id_type=MESH,
        )

    for copy in loads[:parts]:
        copy.wait()
    pl.semaphore_wait(barrier, exps - 1 + dps - 1)

    forwards = dps == 4
    started = []

    def start(copy):
        copy.start()
        started.append(copy)

    def plane_start(k):
        for j in ([1, 2] if forwards else range(1, dps)):
            start(plane_copy(0, j, k, j))

    waited = set()

    def plane_wait(of, k):
        if (of, k) not in waited:
            waited.add((of, k))
            plane_copy(of, of, k, of).wait_recv()

    def forward(k):
        first, then = (1, 2) if k % 2 == 0 else (2, 1)
        plane_wait(first, k)
        start(plane_copy(first, then, k, 3))

    raw[d, e] = block_for(e)
    plane_start(0)
    for k in range(1, exps):
        send[k] = block_for(flip(e, k))
        start(z_copy(k))
    gts[d, e] = gates_for(e)
    for k in range(1, exps):
        gsend[k] = gates_for(flip(e, k))
        start(z_gate(k))

    lag = 2
    for k in range(1, exps):
        z_wait(k)
        plane_start(k)
        if forwards and k >= lag:
            forward(k - lag)
    for k in range(1, exps):
        gate_wait(k)
    for k in range(1, dps):
        start(plane_gate(k))
    loads[parts].wait()
    loads[parts + 1].wait()

    def unpack(at, k):
        src = flip(d, k)
        for g in range(exps // parts):
            arrived = raw[src, pl.ds(g * parts, parts)].reshape(parts * block, cols)
            rr_ = lax.broadcasted_iota(jnp.int32, (block, parts * block), 0)
            cc_ = lax.broadcasted_iota(jnp.int32, (block, parts * block), 1)
            base = (rr_ // most) * block + rr_ % most
            for q in range(parts):
                pick = jnp.where(cc_ == base + q * most, 1.0, 0.0).astype(BF16)
                x[pl.ds(at * rows + g * block, block), pl.ds(q * cols, cols)] = jnp.dot(
                    pick, arrived, preferred_element_type=F32
                ).astype(BF16)

    lane_of = lax.broadcasted_iota(jnp.int32, (rows, LANES), 1)
    row_of = lax.broadcasted_iota(jnp.int32, (rows, LANES), 0)
    own_lane = lane_of == row_of % most

    def gate_column(k):
        src = flip(d, k)
        pick = jnp.where(
            lax.broadcasted_iota(jnp.int32, (rows, exps * 16), 1)
            == (lax.broadcasted_iota(jnp.int32, (rows, exps * 16), 0) // most) * 16,
            1.0, 0.0,
        ).astype(BF16)
        spread = jnp.dot(pick, gts[src].reshape(exps * 16, LANES), preferred_element_type=F32)
        return jnp.sum(jnp.where(own_lane, spread, 0.0), axis=1, keepdims=True)

    tile = min(256, units)
    outs = []

    def compute(ks):
        m = len(ks) * rows
        gates = [gate_column(k) for k in ks]
        starts = [pl.multiple_of(flip(d, k) * rows, 16) for k in ks]
        gacc[pl.ds(0, m), :] = jnp.zeros((m, LANES), F32)

        def body(n, carry):
            at = pl.multiple_of(n * tile, tile)
            back = lax.dot_general(
                x[pl.ds(0, m), :], w[pl.ds(at, tile), :], NT, preferred_element_type=F32
            )
            for i in range(len(ks)):
                part = back[i * rows:(i + 1) * rows]
                ostage[pl.ds(starts[i], rows), pl.ds(at, tile)] = (gates[i] * part).astype(BF16)
                prod = hid[pl.ds(starts[i], rows), pl.ds(at, tile)].astype(F32) * part
                summed = prod[:, :LANES]
                for c in range(1, tile // LANES):
                    summed = summed + prod[:, c * LANES:(c + 1) * LANES]
                gacc[pl.ds(i * rows, rows), :] += summed
            return carry

        lax.fori_loop(0, units // tile, body, 0)
        for i, k in enumerate(ks):
            copy = pltpu.make_async_copy(
                ostage.at[pl.ds(starts[i], rows), :], out_hbm.at[pl.ds(starts[i], rows), :],
                out_sem.at[k],
            )
            copy.start()
            outs.append(copy)
            value = jnp.sum(gacc[pl.ds(i * rows, rows), :], axis=1, keepdims=True)
            spread = jnp.where(own_lane, value, 0.0)
            pick = jnp.where(
                lax.broadcasted_iota(jnp.int32, (exps, rows), 0)
                == lax.broadcasted_iota(jnp.int32, (exps, rows), 1) // most,
                1.0, 0.0,
            )
            psend_buf[k] = jnp.dot(
                pick, spread, preferred_element_type=F32, precision=lax.Precision.HIGHEST
            )
            if k:
                start(sum_copy(k))

    unpack(0, 0)
    if forwards:
        for k in range(exps - lag, exps - 1):
            forward(k)
    compute([0])
    if forwards:
        forward(exps - 1)
    order = list(range(1, dps))
    groups = [order[i:i + 2] for i in range(0, len(order), 2)]
    for group in groups:
        for i, k in enumerate(group):
            plane_gate_wait(k)
            for j in range(exps):
                plane_wait(k, j)
            unpack(i, k)
        compute(group)

    summed = psend_buf[0]
    for k in range(1, dps):
        sum_copy(k).wait_recv()
        summed = summed + precv_buf[k]
    total[...] = summed
    for k in range(1, exps):
        start(back_copy(k))
    erow = lax.broadcasted_iota(jnp.int32, (exps, LANES), 0)
    returned = jnp.zeros((exps, LANES), F32)
    for k in range(exps):
        if k:
            back_copy(k).wait_recv()
            piece = ret[k]
        else:
            piece = summed
        mine = jnp.sum(jnp.where(erow == e, piece, 0.0), axis=0, keepdims=True)
        returned = jnp.where(erow == flip(e, k), mine, returned)
    pick = jnp.where(lax.broadcasted_iota(jnp.int32, (LANES, toks), 0) == slot, 1.0, 0.0)
    spread = jnp.dot(
        returned, pick, preferred_element_type=F32, precision=lax.Precision.HIGHEST
    )
    gg_ref[...] = jnp.sum(spread * onehot, axis=0, keepdims=True)
    for copy in outs:
        copy.wait()
    for copy in started:
        copy.wait_send()


def shards(dps, exps, grad_out, expert_ids, gate_weights, saved_hidden, down_weight):
    toks, width = grad_out.shape
    units = down_weight.shape[1]
    slots = saved_hidden.shape[1]
    most = slots // (dps * exps)
    parts = 16 // math.gcd(most, 16)
    block, cols, rows = parts * most, width // parts, exps * most
    vmem, dma = pltpu.VMEM, pltpu.SemaphoreType.DMA
    any_spec = pl.BlockSpec(memory_space=pl.ANY)
    vm_spec = pl.BlockSpec(memory_space=pltpu.VMEM)
    hidden, gate = pl.pallas_call(
        functools.partial(kernel, dps, exps, most, parts),
        out_shape=(
            jax.ShapeDtypeStruct((slots, units), BF16),
            jax.ShapeDtypeStruct((1, toks), F32),
        ),
        in_specs=[any_spec, vm_spec, vm_spec, any_spec, any_spec],
        out_specs=(any_spec, vm_spec),
        scratch_shapes=[
            vmem((parts * toks, cols), BF16),
            vmem((units, width), BF16),
            vmem((slots, units), BF16),
            vmem((slots, units), BF16),
            vmem((exps, block, cols), BF16),
            vmem((dps, exps, block, cols), BF16),
            vmem((exps, 16, LANES), BF16),
            vmem((dps, exps, 16, LANES), BF16),
            vmem((2 * rows, width), BF16),
            vmem((2 * rows, LANES), F32),
            vmem((dps, exps, LANES), F32),
            vmem((dps, exps, LANES), F32),
            vmem((exps, LANES), F32),
            vmem((exps, exps, LANES), F32),
            dma((parts + 2,)),
            dma((dps,)),
            dma((exps,)), dma((exps,)),
            dma((exps,)), dma((exps,)),
            dma((dps, exps)), dma((dps, exps)),
            dma((dps,)), dma((dps,)),
            dma((dps,)), dma((dps,)),
            dma((exps,)), dma((exps,)),
        ],
        compiler_params=pltpu.CompilerParams(
            collective_id=0, has_side_effects=True, vmem_limit_bytes=58 * 1024 * 1024
        ),
    )(
        grad_out,
        expert_ids.reshape(1, toks),
        gate_weights.reshape(1, toks),
        saved_hidden[0],
        down_weight[0],
    )
    return hidden[None], gate.reshape(toks)


def solution(mesh):
    in_specs = (
        P(("dp", "expert"), None),
        P(("dp", "expert"), None),
        P(("dp", "expert")),
        P("expert", None, "dp"),
        P("expert", "dp", None),
    )
    out_specs = (P("expert", None, "dp"), P(("dp", "expert")))
    body = functools.partial(shards, mesh.shape["dp"], mesh.shape["expert"])
    return jax.shard_map(body, mesh=mesh, in_specs=in_specs, out_specs=out_specs, check_vma=False)
```

time: 207 us -> 100 us (0.48)
  Pallas kernels: 0 us -> 95.4 us
  blocking collectives: 79.3 us -> 0 us
  waiting for transfers between devices: 59.1 us -> 0 us
  matrix products: 23.3 us -> 0 us
  local copies, waits for them, and re-layouts: 23.5 us -> 4.08 us
  between operations: 14.1 us -> 0.65 us
  other arithmetic: 3.78 us -> 0 us
  starting transfers between devices: 3.37 us -> 0 us
    pallas_call x0 -> x1, Pallas kernels: none -> 95.4 us  [shards(): pl.pallas_call(functools.partial(kernel, dps, exps, most, parts), out_sha...]
    all_to_all x2 -> x0, blocking collectives: 62.3 us -> none  [the longest x1 52.4 us: shards(): lax.all_to_all(send_rows, 'expert', split_axis=0, concat_axis=0, tiled=True)]
    all_gather x1 -> x0, waiting for transfers between devices: 53.6 us -> none  [shards(): lax.all_gather(landed_rows[None], 'dp', axis=0, tiled=True)]
    dot_general x3 -> x0, matrix products: 23.3 us -> none  [the longest x1 21.4 us: shards(): lax.dot_general(flat_rows, down_weight[0], (((1,), (1,)), ((), ())), pref...]
    reshape x2 -> x0, local copies, waits for them, and re-layouts: 10.2 us -> none  [the longest x1 8.66 us: shards(): flat_rows = arrived.reshape(-1, width)]
    all_gather x1 -> x0, local copies, waits for them, and re-layouts: 9.63 us -> none  [shards(): lax.all_gather(landed_rows[None], 'dp', axis=0, tiled=True)]
    psum x1 -> x0, blocking collectives: 8.92 us -> none  [shards(): total_gate = lax.psum(partial_gate, 'dp')]
    all_gather x1 -> x0, blocking collectives: 8.08 us -> none  [shards(): lax.all_gather(landed_gates[None], 'dp', axis=0, tiled=True)]
  transfers between devices with their start and end apart: 2 -> 0, of which waited for: 2 -> 0; matrix products, arithmetic and copies ran while one was open for 0% -> 0% of each run, Pallas kernels for 0% -> 0%
where the time goes in v1:
time: 100 us
  Pallas kernels  95.4 us (95%)
  local copies, waits for them, and re-layouts  4.08 us (4%)
    pallas_call x1, Pallas kernels, shards(): pl.pallas_call(functools.partial(kernel, dps, exps, most, parts), out_sha...  95.4 us
    unnamed x4, local copies, waits for them, and re-layouts  4.08 us

profile of v1, /device:TPU:0, one launch (start us, length us, event | category | flops | bytes accessed | tf_op | source)
XLA Modules:
  0.0 100.1 jit_solution(8015340454537503383)
XLA Ops:
  0.6 95.4 %shard_map.68 = (bf16[640,2048]{1,0:T(8,128)(2,1)}, f32[1,128]{1,0:T(1,128)}) custom-call(bf16[128,5120]{1,0:T(8,128)(2,1)} %grad_hbm.1, s32[1,128]{1,0:T(1,128)} %bitcast.9, bf16[1,128]{1,0:T(2,128)(2,1)} %bitcast.10, bf16[640,2048]{1,0:T(8,128)(2,1)} %bitcast.7, bf16[2048,5120]{1,0:T(8,128)(2,1)} %bitcast.6), custom_call_target="tpu_custom_call" | custom-call | tf_op jit(solution)/shard_map/pallas_call | solution.py:329
  96.0 0.0 copy-start
  96.0 3.6 %copy.9 = bf16[1,640,2048]{2,1,0:T(8,128)(2,1)} copy(bf16[1,640,2048]{2,1,0:T(8,128)(2,1)} %bitcast.8) | data formatting | bytes 5242880
  99.6 0.0 copy-done
  99.6 0.5 copy.10
Async XLA Ops:
  96.0 3.6 %copy-start = (f32[1,128]{1,0:T(1,128)S(1)}, f32[1,128]{1,0:T(1,128)}, u32[]{:S(2)}) copy-start(f32[1,128]{1,0:T(1,128)} %get-tuple-element.5) | copy-start | bytes 1540

commit v2 on v1

v2 whole, which is shorter than its diff:
```python
import functools
import math

import jax
import jax.numpy as jnp
from jax import lax
from jax.experimental import pallas as pl
from jax.experimental.pallas import tpu as pltpu
from jax.sharding import PartitionSpec as P

MESH = pl.DeviceIdType.MESH
F32 = jnp.float32
BF16 = jnp.bfloat16
LANES = 128
CHUNKS = (768, 512)
NT = (((1,), (1,)), ((), ()))


def flip(index, mask):
    out, bit = index, 1
    while bit <= mask:
        if mask & bit:
            out = out + bit * (1 - 2 * ((index // bit) % 2))
        bit *= 2
    return out


def kernel(
    dps, exps, most, parts, chunks,
    grad_hbm, ids_ref, gate_ref, hid_hbm, w_hbm,
    out_hbm, gg_ref,
    tokens, w, hid, ostage, *rest,
):
    n = len(chunks)
    send, raw = rest[:n], rest[n:2 * n]
    (
        acc, gsend, gts, x, gacc, psend_buf, precv_buf, total, ret,
        load_sem, out_sem, zs, zr, gzs, gzr, ps, pr, gps, gpr, rs, rr, ts, tr,
    ) = rest[2 * n:]
    offsets = [sum(chunks[:c]) for c in range(n)]
    d = lax.axis_index("dp")
    e = lax.axis_index("expert")
    toks = grad_hbm.shape[0]
    width = grad_hbm.shape[1]
    cols = width // parts
    block = parts * most
    rows = exps * most
    units = w.shape[0]

    loads = [
        pltpu.make_async_copy(
            grad_hbm.at[:, pl.ds(q * cols, cols)],
            tokens.at[pl.ds(q * toks, toks), :],
            load_sem.at[q],
        )
        for q in range(parts)
    ]
    loads.append(pltpu.make_async_copy(w_hbm, w, load_sem.at[parts]))
    loads.append(pltpu.make_async_copy(hid_hbm, hid, load_sem.at[parts + 1]))
    for copy in loads[:parts]:
        copy.start()

    barrier = pltpu.get_barrier_semaphore()
    for k in range(1, exps):
        pl.semaphore_signal(barrier, inc=1, device_id=(d, flip(e, k)), device_id_type=MESH)
    for k in range(1, dps):
        pl.semaphore_signal(barrier, inc=1, device_id=(flip(d, k), e), device_id_type=MESH)

    ids = ids_ref[...]
    onehot = (lax.broadcasted_iota(jnp.int32, (exps, toks), 0) == ids).astype(F32)
    before = (
        lax.broadcasted_iota(jnp.int32, (toks, toks), 0)
        < lax.broadcasted_iota(jnp.int32, (toks, toks), 1)
    )
    earlier = jnp.dot(
        onehot.astype(BF16), before.astype(F32).astype(BF16), preferred_element_type=F32
    )
    slot = jnp.sum(earlier * onehot, axis=0, keepdims=True).astype(jnp.int32)
    target = ids * most + slot

    r4 = lax.broadcasted_iota(jnp.int32, (block, parts * toks), 0)
    c4 = lax.broadcasted_iota(jnp.int32, (block, parts * toks), 1)
    same_part = (r4 // most) == (c4 // toks)
    r_slot = r4 % most
    target4 = jnp.concatenate([target] * parts, axis=1)
    lane_slot = lax.broadcasted_iota(jnp.int32, (LANES, toks), 0)
    gate_rows = jnp.broadcast_to(gate_ref[...].astype(F32), (16, toks)).astype(BF16)

    def block_for(dest, c):
        place = jnp.where(same_part & (r_slot + dest * most == target4), 1.0, 0.0).astype(BF16)
        return jnp.dot(
            place, tokens[:, offsets[c]:offsets[c] + chunks[c]], preferred_element_type=F32
        ).astype(BF16)

    def gates_for(dest):
        hit = (lane_slot < most) & (lane_slot + dest * most == target)
        place = jnp.where(hit, 1.0, 0.0).astype(BF16)
        return lax.dot_general(gate_rows, place, NT, preferred_element_type=F32).astype(BF16)

    def z_copy(c, k):
        dest = flip(e, k)
        return pltpu.make_async_remote_copy(
            src_ref=send[c].at[k], dst_ref=raw[c].at[d, e], send_sem=zs.at[c, k],
            recv_sem=zr.at[c, e],
            device_id=(d, dest), device_id_type=MESH,
        )

    def z_gate(k):
        dest = flip(e, k)
        return pltpu.make_async_remote_copy(
            src_ref=gsend.at[k], dst_ref=gts.at[d, e], send_sem=gzs.at[k], recv_sem=gzr.at[e],
            device_id=(d, dest), device_id_type=MESH,
        )

    def plane_copy(of, via, c, k, j):
        s = flip(e, k)
        src = flip(d, of)
        return pltpu.make_async_remote_copy(
            src_ref=raw[c].at[src, s], dst_ref=raw[c].at[src, s], send_sem=ps.at[c, j, k],
            recv_sem=pr.at[c, src, s], device_id=(flip(d, via), e), device_id_type=MESH,
        )

    def z_wait(c, k):
        s = flip(e, k)
        pltpu.make_async_remote_copy(
            src_ref=send[c].at[k], dst_ref=raw[c].at[d, s], send_sem=zs.at[c, k],
            recv_sem=zr.at[c, s],
            device_id=(d, s), device_id_type=MESH,
        ).wait_recv()

    def gate_wait(k):
        s = flip(e, k)
        pltpu.make_async_remote_copy(
            src_ref=gsend.at[k], dst_ref=gts.at[d, s], send_sem=gzs.at[k], recv_sem=gzr.at[s],
            device_id=(d, s), device_id_type=MESH,
        ).wait_recv()

    def plane_gate(k):
        return pltpu.make_async_remote_copy(
            src_ref=gts.at[d], dst_ref=gts.at[d], send_sem=gps.at[k], recv_sem=gpr.at[d],
            device_id=(flip(d, k), e), device_id_type=MESH,
        )

    def plane_gate_wait(k):
        src = flip(d, k)
        pltpu.make_async_remote_copy(
            src_ref=gts.at[d], dst_ref=gts.at[src], send_sem=gps.at[k], recv_sem=gpr.at[src],
            device_id=(src, e), device_id_type=MESH,
        ).wait_recv()

    def sum_copy(k):
        return pltpu.make_async_remote_copy(
            src_ref=psend_buf.at[k], dst_ref=precv_buf.at[k], send_sem=rs.at[k],
            recv_sem=rr.at[k], device_id=(flip(d, k), e), device_id_type=MESH,
        )

    def back_copy(k):
        return pltpu.make_async_remote_copy(
            src_ref=total, dst_ref=ret.at[k], send_sem=ts.at[k], recv_sem=tr.at[k],
            device_id=(d, flip(e, k)), device_id_type=MESH,
        )

    for copy in loads[:parts]:
        copy.wait()
    for copy in loads[parts:]:
        copy.start()
    raw[0][d, e] = block_for(e, 0)
    pl.semaphore_wait(barrier, exps - 1 + dps - 1)

    forwards = dps == 4
    started = []

    def start(copy):
        copy.start()
        started.append(copy)

    def plane_start(c, k):
        for j in ([1, 2] if forwards else range(1, dps)):
            start(plane_copy(0, j, c, k, j))

    waited = set()

    def plane_wait(of, c, k):
        if (of, c, k) not in waited:
            waited.add((of, c, k))
            plane_copy(of, of, c, k, of).wait_recv()

    def forward(c, k):
        first, then = (1, 2) if k % 2 == 0 else (2, 1)
        plane_wait(first, c, k)
        start(plane_copy(first, then, c, k, 3))

    lane_of = lax.broadcasted_iota(jnp.int32, (block, LANES), 1)
    row_of = lax.broadcasted_iota(jnp.int32, (block, LANES), 0)
    own_lane = lane_of == row_of % most
    tile = min(512 if dps <= 4 else 256, units)
    half = dps * block
    outs = []

    def group(h):
        return flip(e // parts, h)

    def unpack(c, h):
        for k in range(dps):
            for j in range(parts):
                if k:
                    plane_wait(k, c, h * parts + j)
        wide = chunks[c]
        for k in range(dps):
            arrived = raw[c][flip(d, k), pl.ds(group(h) * parts, parts)]
            arrived = arrived.reshape(parts * block, wide)
            rows_ = lax.broadcasted_iota(jnp.int32, (block, parts * block), 0)
            cols_ = lax.broadcasted_iota(jnp.int32, (block, parts * block), 1)
            base = (rows_ // most) * block + rows_ % most
            for q in range(parts):
                pick = jnp.where(cols_ == base + q * most, 1.0, 0.0).astype(BF16)
                x[pl.ds(k * block, block), pl.ds(q * wide, wide)] = jnp.dot(
                    pick, arrived, preferred_element_type=F32
                ).astype(BF16)

    def row_start(h, k):
        return pl.multiple_of(flip(d, k) * rows + group(h) * block, 16)

    def gate_column(h, k):
        pick = jnp.where(
            lax.broadcasted_iota(jnp.int32, (block, parts * 16), 1)
            == (lax.broadcasted_iota(jnp.int32, (block, parts * 16), 0) // most) * 16,
            1.0, 0.0,
        ).astype(BF16)
        tiles = gts[flip(d, k), pl.ds(group(h) * parts, parts)].reshape(parts * 16, LANES)
        spread = jnp.dot(pick, tiles, preferred_element_type=F32)
        return jnp.sum(jnp.where(own_lane, spread, 0.0), axis=1, keepdims=True)

    def compute(c, h, step, gates):
        cols_at = pl.ds(step * tile, tile)
        wide = chunks[c]
        pieces = [w[cols_at, pl.ds(q * cols + offsets[c], wide)] for q in range(parts)]
        weight = jnp.concatenate(pieces, axis=1) if n > 1 else w[cols_at, :]
        back = lax.dot_general(
            x[:, pl.ds(0, parts * wide)], weight, NT, preferred_element_type=F32
        )
        if c:
            back = back + acc[h, :, cols_at]
        if c < n - 1:
            acc[h, :, cols_at] = back
            return
        for k in range(dps):
            part = back[k * block:(k + 1) * block]
            at = pl.ds(row_start(h, k), block)
            ostage[at, cols_at] = (gates[k] * part).astype(BF16)
            prod = hid[at, cols_at].astype(F32) * part
            summed = prod[:, :LANES]
            for i in range(1, tile // LANES):
                summed = summed + prod[:, i * LANES:(i + 1) * LANES]
            if step:
                summed = summed + gacc[h, pl.ds(k * block, block), :]
            gacc[h, pl.ds(k * block, block), :] = summed

    def finish(h):
        for k in range(dps):
            at = pl.ds(row_start(h, k), block)
            copy = pltpu.make_async_copy(ostage.at[at, :], out_hbm.at[at, :], out_sem.at[h, k])
            copy.start()
            outs.append(copy)
        for k in list(range(1, dps)) + [0]:
            value = jnp.sum(gacc[h, pl.ds(k * block, block), :], axis=1, keepdims=True)
            spread = jnp.where(own_lane, value, 0.0)
            pick = jnp.where(
                lax.broadcasted_iota(jnp.int32, (exps, block), 0)
                == group(h) * parts + lax.broadcasted_iota(jnp.int32, (exps, block), 1) // most,
                1.0, 0.0,
            )
            share = jnp.dot(
                pick, spread, preferred_element_type=F32, precision=lax.Precision.HIGHEST
            )
            psend_buf[k] = psend_buf[k] + share if h else share
            if h == halves - 1 and k:
                start(sum_copy(k))

    halves = exps // parts
    steps = units // tile
    work = []
    gates = {}

    def gates_ready():
        loads[parts + 1].wait()
        for k in range(1, dps):
            plane_gate_wait(k)

    def prepare(c, h):
        if c == n - 1:
            gates[h] = [gate_column(h, k) for k in range(dps)]
        unpack(c, h)

    for c in range(n):
        for h in range(halves):
            for step in range(steps):
                work.append((c, h, step))

    def do_work():
        c, h, step = work.pop(0)
        if step == 0:
            if c == 0 and h == 0:
                loads[parts].wait()
            if c == n - 1 and h == 0:
                gates_ready()
            prepare(c, h)
        compute(c, h, step, gates.get(h))
        if c == n - 1 and step == steps - 1:
            finish(h)

    plane_start(0, 0)
    for c in range(n):
        for k in range(exps):
            if k:
                send[c][k] = block_for(flip(e, k), c)
                start(z_copy(c, k))
            elif c:
                raw[c][d, e] = block_for(e, c)
        if c == 0:
            gts[d, e] = gates_for(e)
            for k in range(1, exps):
                gsend[k] = gates_for(flip(e, k))
                start(z_gate(k))

    lag = 2
    order = [(c, k) for c in range(n) for k in range(exps)]
    for i, (c, k) in enumerate(order):
        if i:
            if k:
                z_wait(c, k)
            plane_start(c, k)
        if i == exps - 1:
            for k_ in range(1, exps):
                gate_wait(k_)
            for k_ in range(1, dps):
                start(plane_gate(k_))
        if forwards:
            if i >= lag:
                forward(*order[i - lag])
            if i >= exps and n > 1:
                do_work()
    if forwards:
        for i in range(lag, 0, -1):
            forward(*order[-i])
            if n > 1:
                do_work()
    while work:
        do_work()

    summed = psend_buf[0]
    for k in range(1, dps):
        sum_copy(k).wait_recv()
        summed = summed + precv_buf[k]
    total[...] = summed
    for k in range(1, exps):
        start(back_copy(k))
    erow = lax.broadcasted_iota(jnp.int32, (exps, LANES), 0)
    returned = jnp.zeros((exps, LANES), F32)
    for k in range(exps):
        if k:
            back_copy(k).wait_recv()
            piece = ret[k]
        else:
            piece = summed
        mine = jnp.sum(jnp.where(erow == e, piece, 0.0), axis=0, keepdims=True)
        returned = jnp.where(erow == flip(e, k), mine, returned)
    pick = jnp.where(lax.broadcasted_iota(jnp.int32, (LANES, toks), 0) == slot, 1.0, 0.0)
    spread = jnp.dot(
        returned, pick, preferred_element_type=F32, precision=lax.Precision.HIGHEST
    )
    gg_ref[...] = jnp.sum(spread * onehot, axis=0, keepdims=True)
    for copy in outs:
        copy.wait()
    for copy in started:
        copy.wait_send()


def shards(dps, exps, grad_out, expert_ids, gate_weights, saved_hidden, down_weight):
    toks, width = grad_out.shape
    units = down_weight.shape[1]
    slots = saved_hidden.shape[1]
    most = slots // (dps * exps)
    parts = 16 // math.gcd(most, 16)
    block, cols = parts * most, width // parts
    chunks = CHUNKS if sum(CHUNKS) == cols else (cols,)
    n = len(chunks)
    vmem, dma = pltpu.VMEM, pltpu.SemaphoreType.DMA
    any_spec = pl.BlockSpec(memory_space=pl.ANY)
    vm_spec = pl.BlockSpec(memory_space=pltpu.VMEM)
    hidden, gate = pl.pallas_call(
        functools.partial(kernel, dps, exps, most, parts, chunks),
        out_shape=(
            jax.ShapeDtypeStruct((slots, units), BF16),
            jax.ShapeDtypeStruct((1, toks), F32),
        ),
        in_specs=[any_spec, vm_spec, vm_spec, any_spec, any_spec],
        out_specs=(any_spec, vm_spec),
        scratch_shapes=[
            vmem((parts * toks, cols), BF16),
            vmem((units, width), BF16),
            vmem((slots, units), BF16),
            vmem((slots, units), BF16),
            *[vmem((exps, block, wide), BF16) for wide in chunks],
            *[vmem((dps, exps, block, wide), BF16) for wide in chunks],
            vmem((exps // parts, dps * block, units) if n > 1 else (1, 8, LANES), F32),
            vmem((exps, 16, LANES), BF16),
            vmem((dps, exps, 16, LANES), BF16),
            vmem((dps * block, parts * max(chunks)), BF16),
            vmem((exps // parts, dps * block, LANES), F32),
            vmem((dps, exps, LANES), F32),
            vmem((dps, exps, LANES), F32),
            vmem((exps, LANES), F32),
            vmem((exps, exps, LANES), F32),
            dma((parts + 2,)),
            dma((exps // parts, dps)),
            dma((n, exps)), dma((n, exps)),
            dma((exps,)), dma((exps,)),
            dma((n, dps, exps)), dma((n, dps, exps)),
            dma((dps,)), dma((dps,)),
            dma((dps,)), dma((dps,)),
            dma((exps,)), dma((exps,)),
        ],
        compiler_params=pltpu.CompilerParams(
            collective_id=0, has_side_effects=True, vmem_limit_bytes=58 * 1024 * 1024
        ),
    )(
        grad_out,
        expert_ids.reshape(1, toks),
        gate_weights.reshape(1, toks),
        saved_hidden[0],
        down_weight[0],
    )
    return hidden[None], gate.reshape(toks)


def solution(mesh):
    in_specs = (
        P(("dp", "expert"), None),
        P(("dp", "expert"), None),
        P(("dp", "expert")),
        P("expert", None, "dp"),
        P("expert", "dp", None),
    )
    out_specs = (P("expert", None, "dp"), P(("dp", "expert")))
    body = functools.partial(shards, mesh.shape["dp"], mesh.shape["expert"])
    return jax.shard_map(body, mesh=mesh, in_specs=in_specs, out_specs=out_specs, check_vma=False)
```

time: 100 us -> 89.6 us (0.90)
  Pallas kernels: 95.4 us -> 84.7 us
    pallas_call x1, Pallas kernels: 95.4 us -> 84.7 us  [shards(): pl.pallas_call(functools.partial(kernel, dps, exps, most, parts, chunks),...]
where the time goes in v2:
time: 89.6 us; the launch traced here: 89.4 us
  Pallas kernels  84.7 us (95%)
  local copies, waits for them, and re-layouts  4.08 us (5%)
    pallas_call x1, Pallas kernels, shards(): pl.pallas_call(functools.partial(kernel, dps, exps, most, parts, chunks),...  84.7 us
    unnamed x4, local copies, waits for them, and re-layouts  4.08 us

profile of v2, /device:TPU:0, one launch (start us, length us, event | category | flops | bytes accessed | tf_op | source)
XLA Modules:
  0.0 89.4 jit_solution(11291797684598681997)
XLA Ops:
  0.6 84.7 %shard_map.68 = (bf16[640,2048]{1,0:T(8,128)(2,1)}, f32[1,128]{1,0:T(1,128)}) custom-call(bf16[128,5120]{1,0:T(8,128)(2,1)} %grad_hbm.1, s32[1,128]{1,0:T(1,128)} %bitcast.9, bf16[1,128]{1,0:T(2,128)(2,1)} %bitcast.10, bf16[640,2048]{1,0:T(8,128)(2,1)} %bitcast.7, bf16[2048,5120]{1,0:T(8,128)(2,1)} %bitcast.6), custom_call_target="tpu_custom_call" | custom-call | tf_op jit(solution)/shard_map/pallas_call | solution.py:391
  85.4 0.0 copy-start
  85.4 3.6 %copy.9 = bf16[1,640,2048]{2,1,0:T(8,128)(2,1)} copy(bf16[1,640,2048]{2,1,0:T(8,128)(2,1)} %bitcast.8) | data formatting | bytes 5242880
  88.9 0.0 copy-done
  88.9 0.5 copy.10
Async XLA Ops:
  85.4 3.6 %copy-start = (f32[1,128]{1,0:T(1,128)S(1)}, f32[1,128]{1,0:T(1,128)}, u32[]{:S(2)}) copy-start(f32[1,128]{1,0:T(1,128)} %get-tuple-element.5) | copy-start | bytes 1540
